TPU v7x, 512 devices: a whole 4x8x8 slice. The times are simulated.
512 devices in a mesh: row: 16 (over z, x_lo), col: 32 (over y, x_hi, core).
Axes of the slice: x: 4 (x_hi: 2, x_lo: 2; x = x_hi * 2 + x_lo), y: 8, z: 8, core: 2. Of those that a mesh axis runs over, the one named last changes fastest.
Arguments:
- points: float32 [64, 65536], P(None, ('row', 'col')), may hold values from -6 to 6
- inv_scale: float32 [64], replicated, may hold values from 0.2 to 0.6
- noise_var: float32 [65536], P(('row', 'col')), may hold values from 1 to 16
- residual: float32 [16, 65536], P(None, ('row', 'col')), may hold values from -45 to 45
- direction: float32 [16, 65536], P(None, ('row', 'col')), may hold values from -45 to 45
Outputs:
- residual_next: float32 [16, 65536], P(None, ('row', 'col'))
- direction_next: float32 [16, 65536], P(None, ('row', 'col'))
All inputs are finite; a program needn't handle non-finite values.
Results may differ from a plain program's by a relative error of at most 0.0021.
Values may be sent and summed in bfloat16 or wider, within the bound.
A program may use at most 128 MiB of HBM per device.

v0:
```python
import jax
import jax.numpy as jnp
from jax import lax
from jax.sharding import PartitionSpec as P


def tile_image(row_points, columns, column_norms, column_dirs):
    row_norms = jnp.sum(row_points * row_points, axis=0)
    cross_terms = lax.dot_general(
        row_points,
        columns,
        (((0,), (0,)), ((), ())),
        precision=lax.Precision.HIGHEST,
        preferred_element_type=jnp.float32,
    )
    kernel = jnp.exp(
        -0.5 * (row_norms[:, None] + column_norms[None, :] - 2.0 * cross_terms)
    ).astype(jnp.bfloat16)
    return lax.dot_general(
        column_dirs, kernel, (((1,), (1,)), ((), ())), preferred_element_type=jnp.float32
    )


def on_device(points, inv_scale, noise_var, residual, direction):
    low_dirs = direction.astype(jnp.bfloat16)
    factor = inv_scale[:, None]
    columns = lax.all_gather(points, "row", axis=1, tiled=True) * factor
    column_dirs = lax.all_gather(low_dirs, "row", axis=1, tiled=True)
    column_norms = jnp.sum(columns * columns, axis=0)
    partial_terms = tile_image(
        lax.all_gather(points, "col", axis=1, tiled=True) * factor,
        columns,
        column_norms,
        column_dirs,
    )
    kernel_part = lax.psum_scatter(partial_terms, "col", scatter_dimension=1, tiled=True)
    kernel_image = kernel_part + noise_var[None, :] * direction
    local_norms = jnp.sum(residual * residual, axis=1)
    local_curvature = jnp.sum(direction * kernel_image, axis=1)
    norms_now = lax.psum(local_norms, ("row", "col"))
    curvature = lax.psum(local_curvature, ("row", "col"))
    step_size = norms_now / curvature
    residual_next = residual - step_size[:, None] * kernel_image
    norms_next = lax.psum(jnp.sum(residual_next * residual_next, axis=1), ("row", "col"))
    direction_next = residual_next + (norms_next / norms_now)[:, None] * direction
    return (residual_next, direction_next)


def solution(mesh):
    in_specs = (
        P(None, ("row", "col")),
        P(),
        P(("row", "col")),
        P(None, ("row", "col")),
        P(None, ("row", "col")),
    )
    out_specs = (P(None, ("row", "col")), P(None, ("row", "col")))
    return jax.shard_map(
        on_device, mesh=mesh, in_specs=in_specs, out_specs=out_specs, check_vma=False
    )
```

profile of v0, /device:TPU:1, one launch (start us, length us, event | category | flops | bytes accessed | tf_op | source)
XLA Modules:
  0.0 457.7 jit_solution(1824939552032427751)
XLA Ops:
  7.2 0.0 copy-start.4
  7.2 0.0 all-gather.2.cloned.1.call-start
  7.2 0.7 all-gather.2.cloned.1.call-update
  7.9 0.0 reduce-scatter.2.cloned.1.call-start
  8.0 0.7 convert_element_type.7
  8.7 33.8 %all_gather.11 = bf16[16,2048]{1,0:T(8,128)(2,1)S(1)} all-gather(bf16[16,128]{1,0:T(8,128)(2,1)S(1)} %convert_element_type.7), channel_id=1, replica_groups=mesh['row'=16,'col'=32] {'row'}, dimensions={1}, use_global_device_ids=true | all-gather | bytes 69632 | tf_op jit(solution)/shard_map/all_gather | solution.py:28
  42.4 25.7 %all_gather.10 = f32[64,2048]{1,0:T(8,128)S(1)} all-gather(f32[64,128]{1,0:T(8,128)} %param.5), channel_id=1, replica_groups=mesh['row'=16,'col'=32] {'row'}, dimensions={1}, use_global_device_ids=true | all-gather | bytes 557056 | tf_op jit(solution)/shard_map/all_gather | solution.py:27
  68.2 0.8 multiply_reduce_fusion.1
  69.0 25.4 %all-gather.2.cloned.1.call-done = f32[64,4096]{1,0:T(8,128)} async-done(((f32[64,128]{1,0:T(8,128)}), f32[64,4096]{1,0:T(8,128)}) %all-gather.2.cloned.1.call-update) | async-done | bytes 1048592 | tf_op jit(solution)/shard_map/all_gather | solution.py:31
  94.4 0.0 copy-start
  94.4 31.5 %fusion.2 = f32[4096,2048]{1,0:T(8,128)} fusion(f32[64,4096]{1,0:T(8,128)} %all-gather.2.cloned.1.call-done, f32[64]{0:T(128)} %param.6, f32[64,2048]{1,0:T(8,128)S(1)} %all_gather.10), kind=kOutput, calls=%fused_computation.4 | convolution fusion | flops 6442844160 | bytes 35127552 | tf_op jit(solution)/shard_map/dot_general | solution.py:9
  125.9 0.0 copy-done.4
  125.9 0.0 copy-done
  125.9 0.0 copy-start.3
  125.9 0.0 copy-start.1
  125.9 0.0 copy-start.5
  126.0 0.2 multiply_reduce_fusion
  126.2 15.0 %fusion.1 = f32[16,4096]{1,0:T(8,128)} fusion(bf16[16,2048]{1,0:T(8,128)(2,1)S(1)} %all_gather.11, f32[4096,2048]{1,0:T(8,128)} %fusion.2, f32[2048]{0:T(1024)S(1)} %multiply_reduce_fusion.1, f32[4096]{0:T(1024)S(1)} %multiply_reduce_fusion), kind=kOutput, calls=%fused_computation.2 | convolution fusion | flops 310378496 | bytes 33906688 | tf_op jit(solution)/shard_map/dot_general | solution.py:19
  141.1 0.0 reduce-scatter.2.cloned.1.call-update
  141.2 0.0 copy-done.3
  141.2 0.1 multiply_reduce_fusion.4
  141.3 110.2 %reduce-scatter.2.cloned.1.call-done = f32[16,128]{1,0:T(8,128)} async-done(((f32[16,4096]{1,0:T(8,128)}), f32[16,128]{1,0:T(8,128)}) %reduce-scatter.2.cloned.1.call-update) | async-done | bytes 8208 | tf_op jit(solution)/shard_map/reduce_scatter | solution.py:36
  251.4 0.0 copy-done.1
  251.4 0.0 copy-done.5
  251.4 0.8 multiply_reduce_fusion.3
  252.3 101.9 %all-reduce = (f32[16]{0:T(128)S(1)}, f32[16]{0:T(128)S(1)}) all-reduce(f32[16]{0:T(128)S(1)} %multiply_reduce_fusion.4, f32[16]{0:T(128)S(1)} %multiply_reduce_fusion.3), channel_id=1, replica_groups=mesh['row'=16,'col'=32] {'row','col'}, use_global_device_ids=true, to_apply=%region_1.0 | all-reduce | flops 32 | bytes 256 | tf_op jit(solution)/shard_map/psum | solution.py:40
  354.1 0.9 multiply_reduce_fusion.2
  355.0 0.0 copy-start.2
  355.0 95.2 %psum.23 = f32[16]{0:T(128)S(1)} all-reduce(f32[16]{0:T(128)S(1)} %get-tuple-element.4), channel_id=1, replica_groups=mesh['row'=16,'col'=32] {'row','col'}, use_global_device_ids=true, to_apply=%region_8.0 | all-reduce | flops 16 | bytes 128 | tf_op jit(solution)/shard_map/psum | solution.py:44
  450.2 0.7 multiply_add_fusion
  450.9 0.0 copy-done.2
  (2 shorter events, 0.0 us)
Async XLA Ops:
  7.2 118.8 %copy-start.4 = (f32[64]{0:T(128)S(1)}, f32[64]{0:T(128)}, u32[]{:S(2)}) copy-start(f32[64]{0:T(128)} %param.6) | copy-start | bytes 772
  7.2 87.2 %all-gather.2.cloned.1.call-start = ((), (), s32[]{:S(2)}) async-start(), calls=%async_computation.1 | async-start | bytes 1081344 | tf_op jit(solution)/shard_map/all_gather | solution.py:31
  7.9 243.5 %reduce-scatter.2.cloned.1.call-start = ((), (), s32[]{:S(2)}) async-start(), calls=%async_computation.2 | async-start | bytes 270336 | tf_op jit(solution)/shard_map/reduce_scatter | solution.py:36
  94.4 31.5 %copy-start = (f32[64,4096]{1,0:T(8,128)S(1)}, f32[64,4096]{1,0:T(8,128)}, u32[]{:S(2)}) copy-start(f32[64,4096]{1,0:T(8,128)} %all-gather.2.cloned.1.call-done) | copy-start | bytes 3145732
  125.9 15.2 %copy-start.3 = (f32[16,128]{1,0:T(8,128)S(1)}, f32[16,128]{1,0:T(8,128)}, u32[]{:S(2)}) copy-start(f32[16,128]{1,0:T(8,128)} %param.8) | copy-start | bytes 24580
  125.9 125.5 %copy-start.1 = (f32[16,128]{1,0:T(8,128)S(1)}, f32[16,128]{1,0:T(8,128)}, u32[]{:S(2)}) copy-start(f32[16,128]{1,0:T(8,128)} %param.9) | copy-start | bytes 24580
  125.9 125.5 %copy-start.5 = (f32[128]{0:T(128)S(1)}, f32[128]{0:T(128)}, u32[]{:S(2)}) copy-start(f32[128]{0:T(128)} %param.7) | copy-start | bytes 1540
  355.0 95.8 %copy-start.2 = (f32[16,128]{1,0:T(8,128)}, f32[16,128]{1,0:T(8,128)S(1)}, u32[]{:S(2)}) copy-start(f32[16,128]{1,0:T(8,128)S(1)} %get-tuple-element.5) | copy-start | bytes 24580
Sparse Core Ops, SparseCore 0:
  11.2 83.2 all-gather.1
  141.3 110.1 reduce-scatter.1
where the time goes:
time: 458 us
  blocking collectives  257 us (56%)
  waiting for transfers between devices  136 us (30%)
  matrix products  46.5 us (10%)
  between operations  14.1 us (3%)
    reduce_scatter x1, waiting for transfers between devices, on_device(): lax.psum_scatter(partial_terms, 'col', scatter_dimension=1, tiled=True)  110 us
    psum x1, blocking collectives, on_device(): norms_now = lax.psum(local_norms, ('row', 'col'))  102 us
    psum x1, blocking collectives, on_device(): lax.psum(jnp.sum(residual_next * residual_next, axis=1), ('row', 'col'))  95.2 us
    all_gather x1, blocking collectives, on_device(): column_dirs = lax.all_gather(low_dirs, 'row', axis=1, tiled=True)  33.8 us
    dot_general x1, matrix products, tile_image(): lax.dot_general(row_points, columns, (((0,), (0,)), ((), ())), precision=...  31.5 us
    all_gather x1, blocking collectives, on_device(): columns = lax.all_gather(points, 'row', axis=1, tiled=True) * factor  25.7 us
    all_gather x1, waiting for transfers between devices, on_device(): lax.all_gather(points, 'col', axis=1, tiled=True) * factor  25.4 us
    dot_general x1, matrix products, tile_image(): lax.dot_general(column_dirs, kernel, (((1,), (1,)), ((), ())), preferred_...  15 us
  transfers between devices with their start and end apart: 2, of which 2 were waited for; matrix products, arithmetic and copies ran while one was open for 0% of the time, Pallas kernels for 0%

commit v1 on v0

v1 whole, which is shorter than its diff:
```python
import functools
import math

import jax
import jax.numpy as jnp
from jax import lax
from jax.experimental import pallas as pl
from jax.experimental.pallas import tpu as pltpu
from jax.sharding import PartitionSpec as P

MESH = pl.DeviceIdType.MESH
F = 64
R = 16
B = 128
ROWS, COLS = 16, 32
HALF = COLS // 2
MSG = F + R
DEPTH = 256
KEEP = 48
CODE = 250.0 / 6.0
BIAS = 125.0
SQRT_LOG2E = math.sqrt(math.log2(math.e))
bf16, f32 = jnp.bfloat16, jnp.float32


def encode(x):
    mag = jnp.exp2(jnp.abs(x) * CODE - BIAS)
    return jnp.where(x < 0, -mag, mag).astype(bf16)


def decode(code, factor):
    y = code.astype(f32)
    mag = (jnp.log2(jnp.abs(y)) + BIAS) * factor
    return jnp.where(y < 0, -mag, mag)


def split(a):
    hi = a.astype(bf16)
    hi32 = hi.astype(f32)
    mid = (a - hi32).astype(bf16)
    mid32 = mid.astype(f32)
    norm = -jnp.sum(hi32 * (0.5 * hi32 + mid32), axis=0, keepdims=True)
    n0 = norm.astype(bf16).astype(f32)
    n1 = (norm - n0).astype(bf16).astype(f32)
    n2 = norm - n0 - n1
    return hi, mid, (n0, n1, n2)


def aux_rows(norms, first):
    row = lax.broadcasted_iota(jnp.int32, (16, B), 0)
    out = jnp.where((row >= 3 - first) & (row < 6 - first), 1.0, 0.0)
    for i, n in enumerate(norms):
        out = jnp.where(row == first + i, n, out)
    return out.astype(bf16)


def j_operand(a):
    hi, mid, norms = split(a)
    return jnp.concatenate([hi, mid, hi, mid[:KEEP], aux_rows(norms, 3)], axis=0)


def i_operand(a):
    hi, mid, norms = split(a)
    return jnp.concatenate([hi, hi, mid, mid[:KEEP], aux_rows(norms, 0)], axis=0).T


def kernel(
    points, scale, noise, residual, direction, res_out, dir_out,
    send, jbuf, ibuf, jop, jdir, jacc, obuf, cpart, rpart, sums, csum, sums2, rsum,
    send_sem, jsem, isem, osend, csem, rsem, ssend, ssem, ssem2,
):
    r, c = lax.axis_index("row"), lax.axis_index("col")

    def row_peer(d):
        return (lax.rem(r + d, ROWS), c)

    def col_peer(d):
        return (r, lax.rem(c + d + COLS, COLS))

    def shift(i):
        return jnp.where(lax.rem(i, 2) == 1, i, -i)

    barrier = pltpu.get_barrier_semaphore()

    def greet_row(d, _):
        pl.semaphore_signal(barrier, inc=1, device_id=row_peer(d), device_id_type=MESH)
        return _

    def greet_col(i, _):
        pl.semaphore_signal(barrier, inc=1, device_id=col_peer(shift(i)), device_id_type=MESH)
        return _

    lax.fori_loop(1, ROWS, greet_row, 0)
    lax.fori_loop(1, HALF + 1, greet_col, 0)

    dirs = direction[...]
    send[:F, :] = encode(points[...])
    send[F:, :] = dirs.astype(bf16)
    factor = jnp.broadcast_to(scale[...], (B, F)).T * (SQRT_LOG2E / CODE)

    pl.semaphore_wait(barrier, ROWS - 1 + HALF)

    def to_row(d):
        return pltpu.make_async_remote_copy(
            src_ref=send, dst_ref=jbuf.at[d - 1], send_sem=send_sem, recv_sem=jsem.at[d - 1],
            device_id=row_peer(ROWS - d), device_id_type=MESH)

    def to_col(i):
        return pltpu.make_async_remote_copy(
            src_ref=send, dst_ref=ibuf.at[i - 1], send_sem=send_sem, recv_sem=isem.at[i - 1],
            device_id=col_peer(-shift(i)), device_id_type=MESH)

    def push(k, _):
        @pl.when(k < ROWS)
        def _row():
            to_row(k).start()
        to_col(k).start()
        return _

    lax.fori_loop(1, HALF + 1, push, 0)

    def put_j(d, msg):
        jop[d] = j_operand(decode(msg[:F], factor))
        jdir[d] = msg[F:]
        jacc[d] = jnp.zeros((R, B), f32)

    put_j(0, send[...])

    def take_j(k, _):
        d = jnp.where(lax.rem(k, 2) == 1, lax.div(k + 1, 2), ROWS - lax.div(k, 2))
        to_row(d).wait_recv()
        put_j(d, jbuf[d - 1])
        return _

    lax.fori_loop(1, ROWS, take_j, 0)

    def tile(left, idir, d, both):
        s = jnp.dot(left, jop[d], preferred_element_type=f32)
        p = jnp.exp2(s).astype(bf16)
        if both:
            jacc[d] += jnp.dot(idir, p, preferred_element_type=f32)
        return lax.dot_general(jdir[d], p, (((1,), (1,)), ((), ())), preferred_element_type=f32)

    def i_block(i, msg, one_way, both_ways):
        left = i_operand(decode(msg[:F], factor))
        idir = msg[F:]
        acc = jnp.zeros((R, B), f32)
        for d in range(ROWS):
            if d in one_way or d in both_ways:
                acc += tile(left, idir, d, d in both_ways)
        obuf[i] = acc

    def to_owner(i):
        return pltpu.make_async_remote_copy(
            src_ref=obuf.at[i], dst_ref=cpart.at[i - 1], send_sem=osend, recv_sem=csem,
            device_id=col_peer(shift(i)), device_id_type=MESH)

    half = dict(one_way=(0, ROWS // 2), both_ways=range(1, ROWS // 2))
    i_block(0, send[...], **half)

    def take_i(i, _):
        to_col(i).wait_recv()
        i_block(i, ibuf[i - 1], (), range(ROWS))
        to_owner(i).start()
        return _

    lax.fori_loop(1, HALF, take_i, 0)
    to_col(HALF).wait_recv()
    i_block(HALF, ibuf[HALF - 1], **half)
    to_owner(HALF).start()

    def to_row_owner(d):
        return pltpu.make_async_remote_copy(
            src_ref=jacc.at[d], dst_ref=rpart.at[d - 1], send_sem=osend, recv_sem=rsem,
            device_id=row_peer(d), device_id_type=MESH)

    def push_j(d, _):
        to_row_owner(d).start()
        return _

    lax.fori_loop(1, ROWS, push_j, 0)

    res = residual[...]
    total = obuf[0] + jacc[0] + noise[...] * dirs

    def whole(src, dst, s_sem, r_sem):
        return pltpu.make_async_remote_copy(
            src_ref=src, dst_ref=dst, send_sem=s_sem, recv_sem=r_sem,
            device_id=row_peer(1), device_id_type=MESH)

    whole(cpart, cpart, osend, csem).wait_recv()
    total += jnp.sum(cpart[...], axis=0)
    whole(rpart, rpart, osend, rsem).wait_recv()
    image = total + jnp.sum(rpart[...], axis=0)

    lane = lax.broadcasted_iota(jnp.int32, (R, B), 1)
    local = jnp.zeros((R, B), f32)
    for n, prod in enumerate((res * res, res * image, dirs * image, image * image)):
        local = jnp.where(lane == n, jnp.sum(prod, axis=1, keepdims=True), local)
    sums[...] = local

    def sum_to_col(d):
        return pltpu.make_async_remote_copy(
            src_ref=sums, dst_ref=csum.at[d - 1], send_sem=ssend, recv_sem=ssem,
            device_id=col_peer(d), device_id_type=MESH)

    def push_c(d, _):
        sum_to_col(d).start()
        return _

    lax.fori_loop(1, COLS, push_c, 0)
    whole(csum, csum, ssend, ssem).wait_recv()
    sums2[...] = sums[...] + jnp.sum(csum[...], axis=0)

    def sum_to_row(d):
        return pltpu.make_async_remote_copy(
            src_ref=sums2, dst_ref=rsum.at[d - 1], send_sem=ssend, recv_sem=ssem2,
            device_id=row_peer(d), device_id_type=MESH)

    def push_r(d, _):
        sum_to_row(d).start()
        return _

    lax.fori_loop(1, ROWS, push_r, 0)
    whole(rsum, rsum, ssend, ssem2).wait_recv()
    tot = sums2[...] + jnp.sum(rsum[...], axis=0)
    rr, rq, dq, qq = tot[:, 0:1], tot[:, 1:2], tot[:, 2:3], tot[:, 3:4]
    step = rr / dq
    nxt = rr - 2.0 * step * rq + step * (step * qq)
    res_next = res - step * image
    res_out[...] = res_next
    dir_out[...] = res_next + (nxt / rr) * dirs

    whole(jbuf, jbuf, send_sem, jsem.at[0]).wait_send()
    whole(ibuf, ibuf, send_sem, jsem.at[0]).wait_send()
    whole(cpart, cpart, osend, csem).wait_send()
    whole(rpart, rpart, osend, rsem).wait_send()
    whole(csum, csum, ssend, ssem).wait_send()
    whole(rsum, rsum, ssend, ssem2).wait_send()


def on_device(points, inv_scale, noise_var, residual, direction):
    vmem = pl.BlockSpec(memory_space=pltpu.VMEM)
    dma = pltpu.SemaphoreType.DMA
    out = jax.ShapeDtypeStruct((R, B), f32)
    return pl.pallas_call(
        kernel,
        out_shape=(out, out),
        in_specs=[vmem] * 5,
        out_specs=(vmem, vmem),
        scratch_shapes=[
            pltpu.VMEM((MSG, B), bf16),
            pltpu.VMEM((ROWS - 1, MSG, B), bf16),
            pltpu.VMEM((HALF, MSG, B), bf16),
            pltpu.VMEM((ROWS, DEPTH, B), bf16),
            pltpu.VMEM((ROWS, R, B), bf16),
            pltpu.VMEM((ROWS, R, B), f32),
            pltpu.VMEM((HALF + 1, R, B), f32),
            pltpu.VMEM((HALF, R, B), f32),
            pltpu.VMEM((ROWS - 1, R, B), f32),
            pltpu.VMEM((R, B), f32),
            pltpu.VMEM((COLS - 1, R, B), f32),
            pltpu.VMEM((R, B), f32),
            pltpu.VMEM((ROWS - 1, R, B), f32),
            dma, dma((ROWS - 1,)), dma((HALF,)), dma, dma, dma, dma, dma, dma,
        ],
        compiler_params=pltpu.CompilerParams(
            collective_id=0, has_side_effects=True, vmem_limit_bytes=32 << 20),
    )(points, inv_scale.reshape(1, F), noise_var.reshape(1, B), residual, direction)


def solution(mesh):
    split_points = P(None, ("row", "col"))
    return jax.shard_map(
        on_device,
        mesh=mesh,
        in_specs=(split_points, P(), P(("row", "col")), split_points, split_points),
        out_specs=(split_points, split_points),
        check_vma=False,
    )
```

time: 458 us -> 87.7 us (0.19)
  blocking collectives: 257 us -> 0 us
  waiting for transfers between devices: 136 us -> 0 us
  Pallas kernels: 0 us -> 81.9 us
  matrix products: 46.5 us -> 0 us
  between operations: 14.1 us -> 0.66 us
    psum x2 -> x0, blocking collectives: 197 us -> none  [the longest x1 102 us: on_device(): norms_now = lax.psum(local_norms, ('row', 'col'))]
    reduce_scatter x1 -> x0, waiting for transfers between devices: 110 us -> none  [on_device(): lax.psum_scatter(partial_terms, 'col', scatter_dimension=1, tiled=True)]
    pallas_call x0 -> x1, Pallas kernels: none -> 81.9 us  [on_device(): pl.pallas_call(kernel, out_shape=(out, out), in_specs=[vmem] * 5, out_spe...]
    all_gather x2 -> x0, blocking collectives: 59.5 us -> none  [the longest x1 33.8 us: on_device(): column_dirs = lax.all_gather(low_dirs, 'row', axis=1, tiled=True)]
    dot_general x2 -> x0, matrix products: 46.5 us -> none  [the longest x1 31.5 us: tile_image(): lax.dot_general(row_points, columns, (((0,), (0,)), ((), ())), precision=...]
    all_gather x1 -> x0, waiting for transfers between devices: 25.4 us -> none  [on_device(): lax.all_gather(points, 'col', axis=1, tiled=True) * factor]
  transfers between devices with their start and end apart: 2 -> 0, of which waited for: 2 -> 0; matrix products, arithmetic and copies ran while one was open for 0% -> 0% of each run, Pallas kernels for 0% -> 0%
where the time goes in v1:
time: 87.7 us; the launch traced here: 86.5 us
  Pallas kernels  81.9 us (93%)
  local copies, waits for them, and re-layouts  4 us (5%)
    pallas_call x1, Pallas kernels, on_device(): pl.pallas_call(kernel, out_shape=(out, out), in_specs=[vmem] * 5, out_spe...  81.9 us
    unnamed x12, local copies, waits for them, and re-layouts  4 us

profile of v1, /device:TPU:1, one launch (start us, length us, event | category | flops | bytes accessed | tf_op | source)
XLA Modules:
  0.0 86.5 jit_solution(13020391358329960129)
XLA Ops:
  0.6 0.0 copy-start.3
  0.6 0.0 copy-start.4
  0.7 0.6 copy-done.3
  1.3 0.0 copy-done.4
  1.3 0.0 copy-start
  1.3 0.8 copy-done
  2.1 0.0 copy-start.1
  2.1 0.7 copy-done.1
  2.8 0.0 copy-start.2
  2.8 0.7 copy-done.2
  3.5 81.9 %shard_map.68 = (f32[16,128]{1,0:T(8,128)S(1)}, f32[16,128]{1,0:T(8,128)S(1)}) custom-call(f32[64,128]{1,0:T(8,128)S(1)} %copy-done, f32[1,64]{1,0:T(1,128)S(1)} %bitcast.2, f32[1,128]{1,0:T(1,128)S(1)} %bitcast.3, f32[16,128]{1,0:T(8,128)S(1)} %copy-done.1, f32[16,128]{1,0:T(8,128)S(1)} %copy-done.2), custom_call_target="tpu_custom_call" | custom-call | tf_op jit(solution)/shard_map/pallas_call | solution.py:246
  85.3 0.6 copy.9
  86.0 0.6 copy.10
Async XLA Ops:
  0.6 0.7 copy-start.3
  0.6 0.7 copy-start.4
  1.3 0.8 copy-start
  2.1 0.7 copy-start.1
  2.8 0.7 copy-start.2

commit v2 on v1

--- a/solution.py
+++ b/solution.py
@@ -17,6 +17,7 @@
 MSG = F + R
 DEPTH = 256
 KEEP = 48
+CHUNK = 512
 CODE = 250.0 / 6.0
 BIAS = 125.0
 SQRT_LOG2E = math.sqrt(math.log2(math.e))
@@ -47,7 +48,7 @@
 
 
 def aux_rows(norms, first):
-    row = lax.broadcasted_iota(jnp.int32, (16, B), 0)
+    row = lax.broadcasted_iota(jnp.int32, (16, norms[0].shape[1]), 0)
     out = jnp.where((row >= 3 - first) & (row < 6 - first), 1.0, 0.0)
     for i, n in enumerate(norms):
         out = jnp.where(row == first + i, n, out)
@@ -66,7 +67,7 @@
 
 def kernel(
     points, scale, noise, residual, direction, res_out, dir_out,
-    send, jbuf, ibuf, jop, jdir, jacc, obuf, cpart, rpart, sums, csum, sums2, rsum,
+    send, jbuf, ibuf, jop, jdir, jacc, probs, obuf, cpart, rpart, sums, csum, sums2, rsum,
     send_sem, jsem, isem, osend, csem, rsem, ssend, ssem, ssem2,
 ):
     r, c = lax.axis_index("row"), lax.axis_index("col")
@@ -96,7 +97,7 @@
     dirs = direction[...]
     send[:F, :] = encode(points[...])
     send[F:, :] = dirs.astype(bf16)
-    factor = jnp.broadcast_to(scale[...], (B, F)).T * (SQRT_LOG2E / CODE)
+    factor = jnp.broadcast_to(scale[...], (B, F)).T[:, :1] * (SQRT_LOG2E / CODE)
 
     pl.semaphore_wait(barrier, ROWS - 1 + HALF)
 
@@ -119,10 +120,12 @@
 
     lax.fori_loop(1, HALF + 1, push, 0)
 
+    def slot(d):
+        return pl.ds(pl.multiple_of(d * B, B), B)
+
     def put_j(d, msg):
-        jop[d] = j_operand(decode(msg[:F], factor))
-        jdir[d] = msg[F:]
-        jacc[d] = jnp.zeros((R, B), f32)
+        jop[:, slot(d)] = j_operand(decode(msg[:F], factor))
+        jdir[:, slot(d)] = msg[F:]
 
     put_j(0, send[...])
 
@@ -134,44 +137,46 @@
 
     lax.fori_loop(1, ROWS, take_j, 0)
 
-    def tile(left, idir, d, both):
-        s = jnp.dot(left, jop[d], preferred_element_type=f32)
-        p = jnp.exp2(s).astype(bf16)
-        if both:
-            jacc[d] += jnp.dot(idir, p, preferred_element_type=f32)
-        return lax.dot_general(jdir[d], p, (((1,), (1,)), ((), ())), preferred_element_type=f32)
-
-    def i_block(i, msg, one_way, both_ways):
-        left = i_operand(decode(msg[:F], factor))
-        idir = msg[F:]
-        acc = jnp.zeros((R, B), f32)
-        for d in range(ROWS):
-            if d in one_way or d in both_ways:
-                acc += tile(left, idir, d, d in both_ways)
-        obuf[i] = acc
+    def tiles(points_i, dirs_i, probs):
+        left = i_operand(decode(points_i, factor))
+        for n in range(ROWS * B // CHUNK):
+            part = pl.ds(n * CHUNK, CHUNK)
+            s = jnp.dot(left, jop[:, part], preferred_element_type=f32)
+            probs[:, part] = jnp.exp2(s).astype(bf16)
+        out = lax.dot_general(jdir[...], probs[...], (((1,), (1,)), ((), ())), preferred_element_type=f32)
+        return out, jnp.dot(dirs_i, probs[...], preferred_element_type=f32)
 
     def to_owner(i):
         return pltpu.make_async_remote_copy(
             src_ref=obuf.at[i], dst_ref=cpart.at[i - 1], send_sem=osend, recv_sem=csem,
             device_id=col_peer(shift(i)), device_id_type=MESH)
 
-    half = dict(one_way=(0, ROWS // 2), both_ways=range(1, ROWS // 2))
-    i_block(0, send[...], **half)
-
-    def take_i(i, _):
+    out, more = tiles(send[:F], send[F:] * bf16(0.5), probs.at[:B])
+    obuf[0] = out * 0.5
+    jacc[...] = more
+
+    def take_i(q, _):
+        i = 2 * q + 1
         to_col(i).wait_recv()
-        i_block(i, ibuf[i - 1], (), range(ROWS))
+        to_col(i + 1).wait_recv()
+        weight = jnp.where(q == HALF // 2 - 1, 0.5, 1.0)
+        first, second = ibuf[i - 1], ibuf[i]
+        halved = (second[F:].astype(f32) * weight).astype(bf16)
+        out, more = tiles(
+            jnp.concatenate([first[:F], second[:F]], axis=1),
+            jnp.concatenate([first[F:], halved], axis=1), probs)
+        obuf[i] = out[:, :B]
+        obuf[i + 1] = out[:, B:] * weight
+        jacc[...] += more
         to_owner(i).start()
-        return _
-
-    lax.fori_loop(1, HALF, take_i, 0)
-    to_col(HALF).wait_recv()
-    i_block(HALF, ibuf[HALF - 1], **half)
-    to_owner(HALF).start()
+        to_owner(i + 1).start()
+        return _
+
+    lax.fori_loop(0, HALF // 2, take_i, 0)
 
     def to_row_owner(d):
         return pltpu.make_async_remote_copy(
-            src_ref=jacc.at[d], dst_ref=rpart.at[d - 1], send_sem=osend, recv_sem=rsem,
+            src_ref=jacc.at[:, slot(d)], dst_ref=rpart.at[d - 1], send_sem=osend, recv_sem=rsem,
             device_id=row_peer(d), device_id_type=MESH)
 
     def push_j(d, _):
@@ -181,7 +186,7 @@
     lax.fori_loop(1, ROWS, push_j, 0)
 
     res = residual[...]
-    total = obuf[0] + jacc[0] + noise[...] * dirs
+    total = obuf[0] + jacc[:, :B] + noise[...] * dirs
 
     def whole(src, dst, s_sem, r_sem):
         return pltpu.make_async_remote_copy(
@@ -252,9 +257,10 @@
             pltpu.VMEM((MSG, B), bf16),
             pltpu.VMEM((ROWS - 1, MSG, B), bf16),
             pltpu.VMEM((HALF, MSG, B), bf16),
-            pltpu.VMEM((ROWS, DEPTH, B), bf16),
-            pltpu.VMEM((ROWS, R, B), bf16),
-            pltpu.VMEM((ROWS, R, B), f32),
+            pltpu.VMEM((DEPTH, ROWS * B), bf16),
+            pltpu.VMEM((R, ROWS * B), bf16),
+            pltpu.VMEM((R, ROWS * B), f32),
+            pltpu.VMEM((2 * B, ROWS * B), bf16),
             pltpu.VMEM((HALF + 1, R, B), f32),
             pltpu.VMEM((HALF, R, B), f32),
             pltpu.VMEM((ROWS - 1, R, B), f32),

time: 87.7 us -> 61.7 us (0.70)
  the two profiles are of different devices: /device:TPU:1 before, /device:TPU:4 now
where the time goes in v2:
time: 61.7 us; the launch traced here: 61.4 us
  Pallas kernels  56.8 us (92%)
  local copies, waits for them, and re-layouts  4 us (6%)
  between operations  0.66 us (1%)
    pallas_call x1, Pallas kernels, on_device(): pl.pallas_call(kernel, out_shape=(out, out), in_specs=[vmem] * 5, out_spe...  56.8 us
    unnamed x12, local copies, waits for them, and re-layouts  4 us

profile of v2, /device:TPU:4, one launch (start us, length us, event | category | flops | bytes accessed | tf_op | source)
XLA Modules:
  0.0 61.4 jit_solution(12958807056284002824)
XLA Ops:
  0.6 0.0 copy-start.3
  0.6 0.0 copy-start.4
  0.7 0.6 %copy-done.3 = f32[64]{0:T(128)S(1)} copy-done((f32[64]{0:T(128)S(1)}, f32[64]{0:T(128)}, u32[]{:S(2)}) %copy-start.3) | copy-done | bytes 280
  1.3 0.0 copy-done.4
  1.3 0.0 copy-start
  1.3 0.8 %copy-done = f32[64,128]{1,0:T(8,128)S(1)} copy-done((f32[64,128]{1,0:T(8,128)S(1)}, f32[64,128]{1,0:T(8,128)}, u32[]{:S(2)}) %copy-start) | copy-done | bytes 32792
  2.1 0.0 copy-start.1
  2.1 0.7 %copy-done.1 = f32[16,128]{1,0:T(8,128)S(1)} copy-done((f32[16,128]{1,0:T(8,128)S(1)}, f32[16,128]{1,0:T(8,128)}, u32[]{:S(2)}) %copy-start.1) | copy-done | bytes 8216
  2.8 0.0 copy-start.2
  2.8 0.7 %copy-done.2 = f32[16,128]{1,0:T(8,128)S(1)} copy-done((f32[16,128]{1,0:T(8,128)S(1)}, f32[16,128]{1,0:T(8,128)}, u32[]{:S(2)}) %copy-start.2) | copy-done | bytes 8216
  3.5 56.8 %shard_map.68 = (f32[16,128]{1,0:T(8,128)S(1)}, f32[16,128]{1,0:T(8,128)S(1)}) custom-call(f32[64,128]{1,0:T(8,128)S(1)} %copy-done, f32[1,64]{1,0:T(1,128)S(1)} %bitcast.2, f32[1,128]{1,0:T(1,128)S(1)} %bitcast.3, f32[16,128]{1,0:T(8,128)S(1)} %copy-done.1, f32[16,128]{1,0:T(8,128)S(1)} %copy-done.2), custom_call_target="tpu_custom_call" | custom-call | tf_op jit(solution)/shard_map/pallas_call | solution.py:251
  60.2 0.6 copy.9
  60.8 0.6 copy.10
Async XLA Ops:
  0.6 0.7 %copy-start.3 = (f32[64]{0:T(128)S(1)}, f32[64]{0:T(128)}, u32[]{:S(2)}) copy-start(f32[64]{0:T(128)} %param.6) | copy-start | bytes 772
  0.6 0.7 %copy-start.4 = (f32[128]{0:T(128)S(1)}, f32[128]{0:T(128)}, u32[]{:S(2)}) copy-start(f32[128]{0:T(128)} %param.7) | copy-start | bytes 1540
  1.3 0.8 %copy-start = (f32[64,128]{1,0:T(8,128)S(1)}, f32[64,128]{1,0:T(8,128)}, u32[]{:S(2)}) copy-start(f32[64,128]{1,0:T(8,128)} %points.1) | copy-start | bytes 98308
  2.1 0.7 %copy-start.1 = (f32[16,128]{1,0:T(8,128)S(1)}, f32[16,128]{1,0:T(8,128)}, u32[]{:S(2)}) copy-start(f32[16,128]{1,0:T(8,128)} %residual.1) | copy-start | bytes 24580
  2.8 0.7 %copy-start.2 = (f32[16,128]{1,0:T(8,128)S(1)}, f32[16,128]{1,0:T(8,128)}, u32[]{:S(2)}) copy-start(f32[16,128]{1,0:T(8,128)} %direction.1) | copy-start | bytes 24580

commit v3 on v2

v3 whole, which is shorter than its diff:
```python
import functools
import math

import jax
import jax.numpy as jnp
from jax import lax
from jax.experimental import pallas as pl
from jax.experimental.pallas import tpu as pltpu
from jax.sharding import PartitionSpec as P

MESH = pl.DeviceIdType.MESH
F = 64
R = 16
B = 128
ROWS, COLS = 16, 32
HALF = COLS // 2
MSG = F + R
DEPTH = 256
KEEP = 48
GROUP, GROUPS = 4, 4
WIDTH = ROWS * B // 2
CHUNK = 512
CODE = 250.0 / 6.0
BIAS = 125.0
SQRT_LOG2E = math.sqrt(math.log2(math.e))
bf16, f32 = jnp.bfloat16, jnp.float32


def encode(x):
    mag = jnp.exp2(jnp.abs(x) * CODE - BIAS)
    return jnp.where(x < 0, -mag, mag).astype(bf16)


def decode(code, factor):
    y = code.astype(f32)
    mag = (jnp.log2(jnp.abs(y)) + BIAS) * factor
    return jnp.where(y < 0, -mag, mag)


def split(a):
    hi = a.astype(bf16)
    hi32 = hi.astype(f32)
    mid = (a - hi32).astype(bf16)
    mid32 = mid.astype(f32)
    norm = -jnp.sum(hi32 * (0.5 * hi32 + mid32), axis=0, keepdims=True)
    n0 = norm.astype(bf16).astype(f32)
    n1 = (norm - n0).astype(bf16).astype(f32)
    n2 = norm - n0 - n1
    return hi, mid, (n0, n1, n2)


def aux_rows(norms, first):
    row = lax.broadcasted_iota(jnp.int32, (16, norms[0].shape[1]), 0)
    out = jnp.where((row >= 3 - first) & (row < 6 - first), 1.0, 0.0)
    for i, n in enumerate(norms):
        out = jnp.where(row == first + i, n, out)
    return out.astype(bf16)


def j_operand(a):
    hi, mid, norms = split(a)
    return jnp.concatenate([hi, mid, hi, mid[:KEEP], aux_rows(norms, 3)], axis=0)


def i_operand(a):
    hi, mid, norms = split(a)
    return jnp.concatenate([hi, hi, mid, mid[:KEEP], aux_rows(norms, 0)], axis=0).T


def far_first(k, n):
    return jnp.where(lax.rem(k, 2) == 1, n // 2 - lax.div(k, 2), n // 2 + lax.div(k, 2))


def kernel(
    points_hbm, scale_hbm, noise_hbm, residual_hbm, direction_hbm, res_out, dir_out,
    points, scale, noise, residual, direction, send, jbuf, ibuf, jop, jdir, jacc, iop, idir, oown, own, probs, obuf, cpart, rpart, sums, csum, sums2, rsum,
    in_sem, send_sem, jsem, isem, osend, csem, rsem, ssend, ssem, ssem2,
):
    r, c = lax.axis_index("row"), lax.axis_index("col")

    def row_peer(d):
        return (lax.rem(r + d, ROWS), c)

    def col_peer(d):
        return (r, lax.rem(c + d + COLS, COLS))

    def shift(i):
        return jnp.where(lax.rem(i, 2) == 1, i, -i)

    staged = ((points_hbm, points), (scale_hbm, scale), (noise_hbm, noise), (residual_hbm, residual), (direction_hbm, direction))
    for n, (src, dst) in enumerate(staged):
        pltpu.make_async_copy(src, dst, in_sem.at[n]).start()

    barrier = pltpu.get_barrier_semaphore()

    def greet(k, _):
        @pl.when(k < ROWS)
        def _row():
            pl.semaphore_signal(barrier, inc=1, device_id=row_peer(far_first(k, ROWS)), device_id_type=MESH)
        i = HALF + 1 - k
        pl.semaphore_signal(barrier, inc=1, device_id=col_peer(shift(i)), device_id_type=MESH)
        return _

    lax.fori_loop(1, HALF + 1, greet, 0)

    for n, (src, dst) in enumerate(staged):
        pltpu.make_async_copy(src, dst, in_sem.at[n]).wait()
    dirs = direction[...]
    send[:F, :] = encode(points[...])
    send[F:, :] = dirs.astype(bf16)
    factor = jnp.broadcast_to(scale[...], (B, F)).T[:, :1] * (SQRT_LOG2E / CODE)

    pl.semaphore_wait(barrier, ROWS - 1 + HALF)

    def to_row(d):
        return pltpu.make_async_remote_copy(
            src_ref=send, dst_ref=jbuf.at[d - 1], send_sem=send_sem, recv_sem=jsem.at[d - 1],
            device_id=row_peer(ROWS - d), device_id_type=MESH)

    def to_col(i):
        return pltpu.make_async_remote_copy(
            src_ref=send, dst_ref=ibuf.at[i - 1], send_sem=send_sem, recv_sem=isem.at[i - 1],
            device_id=col_peer(-shift(i)), device_id_type=MESH)

    def near_first(p):
        return jnp.where(lax.rem(p, 2) == 1, lax.div(p + 1, 2), lax.rem(ROWS - lax.div(p, 2), ROWS))

    def push(k, _):
        @pl.when(k < ROWS)
        def _row():
            to_row(near_first(k)).start()
        to_col(k).start()
        return _

    lax.fori_loop(1, HALF + 1, push, 0)

    def slot(n):
        return pl.ds(pl.multiple_of(n * B, B), B)

    def put_j(p, msg):
        part, place = lax.div(p, ROWS // 2), slot(lax.rem(p, ROWS // 2))
        jop[part, :, place] = j_operand(decode(msg[:F], factor))
        jdir[part, :, place] = msg[F:]

    def take_j(p, _):
        d = near_first(p)
        to_row(d).wait_recv()
        put_j(p, jbuf[d - 1])
        return _

    def take_i(n, g):
        i = g * GROUP + n
        to_col(i + 1).wait_recv()
        msg = ibuf[i]
        weight = jnp.where(i == HALF - 1, 0.5, 1.0)
        iop[g, slot(n), :] = i_operand(decode(msg[:F], factor))
        idir[g, :, slot(n)] = (msg[F:].astype(f32) * weight).astype(bf16)
        return g

    def tile(left, dirs_i, h, probs):
        for n in range(WIDTH // CHUNK):
            part = pl.ds(n * CHUNK, CHUNK)
            s = jnp.dot(left, jop[h, :, part], preferred_element_type=f32)
            probs[:, part] = jnp.exp2(s).astype(bf16)
        jacc[h] += jnp.dot(dirs_i, probs[...], preferred_element_type=f32)
        return lax.dot_general(jdir[h], probs[...], (((1,), (1,)), ((), ())), preferred_element_type=f32)

    def to_owner(n, g):
        i = g * GROUP + n
        return pltpu.make_async_remote_copy(
            src_ref=obuf.at[g, :, slot(n)], dst_ref=cpart.at[i], send_sem=osend, recv_sem=csem,
            device_id=col_peer(shift(i + 1)), device_id_type=MESH)

    def push_o(n, g):
        to_owner(n, g).start()
        return g

    def to_row_owner(p):
        d = near_first(p)
        return pltpu.make_async_remote_copy(
            src_ref=jacc.at[lax.div(p, ROWS // 2), :, slot(lax.rem(p, ROWS // 2))], dst_ref=rpart.at[d - 1],
            send_sem=osend, recv_sem=rsem, device_id=row_peer(d), device_id_type=MESH)

    def push_j(p, _):
        to_row_owner(p).start()
        return _

    put_j(0, send[...])
    oown[...] = i_operand(decode(send[:F], factor))
    jacc[...] = jnp.zeros(jacc.shape, f32)
    obuf[...] = jnp.zeros(obuf.shape, f32)
    own[...] = jnp.zeros(own.shape, f32)

    def step_of(t, _):
        early = t < GROUPS
        g = jnp.where(early, lax.rem(t, 2), lax.div(t, 2))
        h = jnp.where(early, lax.div(t, 2), lax.rem(t, 2))

        @pl.when(early & (lax.rem(t, 2) == 0))
        def _half():
            lax.fori_loop(jnp.maximum(h * (ROWS // 2), 1), (h + 1) * (ROWS // 2), take_j, 0)
            own[...] += 0.5 * tile(oown[...], send[F:] * bf16(0.5), h, probs.at[:B])

        @pl.when(h == 0)
        def _group():
            lax.fori_loop(0, GROUP, take_i, g)

        obuf[g] += tile(iop[g], idir[g], h, probs)

        @pl.when(t == 2 * GROUPS - 1)
        def _last():
            obuf[g, :, slot(GROUP - 1)] = 0.5 * obuf[g, :, slot(GROUP - 1)]

        @pl.when(h == 1)
        def _rows_done():
            lax.fori_loop(0, GROUP, push_o, g)

        @pl.when(t >= 2 * GROUPS - 2)
        def _columns_done():
            lax.fori_loop(jnp.maximum(h * (ROWS // 2), 1), (h + 1) * (ROWS // 2), push_j, 0)
        return _

    lax.fori_loop(0, 2 * GROUPS, step_of, 0)

    res = residual[...]
    total = own[...] + jacc[0, :, :B] + noise[...] * dirs

    def whole(src, dst, s_sem, r_sem):
        return pltpu.make_async_remote_copy(
            src_ref=src, dst_ref=dst, send_sem=s_sem, recv_sem=r_sem,
            device_id=row_peer(1), device_id_type=MESH)

    whole(cpart, cpart, osend, csem).wait_recv()
    total += jnp.sum(cpart[...], axis=0)
    whole(rpart, rpart, osend, rsem).wait_recv()
    image = total + jnp.sum(rpart[...], axis=0)

    ahead = lax.broadcasted_iota(jnp.int32, (R, B), 1) - lax.broadcasted_iota(jnp.int32, (R, B), 0)
    local = jnp.zeros((R, B), f32)
    for n, prod in enumerate((res * res, res * image, dirs * image, image * image)):
        local = jnp.where(ahead == n * R, jnp.sum(prod, axis=1, keepdims=True), local)
    sums[...] = jnp.sum(local, axis=0, keepdims=True)

    def sum_to_col(d):
        return pltpu.make_async_remote_copy(
            src_ref=sums, dst_ref=csum.at[pl.ds(d - 1, 1)], send_sem=ssend, recv_sem=ssem,
            device_id=col_peer(d), device_id_type=MESH)

    def push_c(k, _):
        sum_to_col(far_first(k, COLS)).start()
        return _

    lax.fori_loop(1, COLS, push_c, 0)
    whole(csum, csum, ssend, ssem).wait_recv()
    sums2[...] = sums[...] + jnp.sum(csum[...], axis=0, keepdims=True)

    def sum_to_row(d):
        return pltpu.make_async_remote_copy(
            src_ref=sums2, dst_ref=rsum.at[pl.ds(d - 1, 1)], send_sem=ssend, recv_sem=ssem2,
            device_id=row_peer(d), device_id_type=MESH)

    def push_r(k, _):
        sum_to_row(far_first(k, ROWS)).start()
        return _

    lax.fori_loop(1, ROWS, push_r, 0)
    whole(rsum, rsum, ssend, ssem2).wait_recv()
    tot = sums2[...] + jnp.sum(rsum[...], axis=0, keepdims=True)
    rr, rq, dq, qq = (jnp.sum(jnp.where(ahead == n * R, tot, 0.0), axis=1, keepdims=True) for n in range(4))
    step = rr / dq
    nxt = rr - 2.0 * step * rq + step * (step * qq)
    res_next = res - step * image
    res_out[...] = res_next
    dir_out[...] = res_next + (nxt / rr) * dirs

    whole(jbuf, jbuf, send_sem, jsem.at[0]).wait_send()
    whole(ibuf, ibuf, send_sem, jsem.at[0]).wait_send()
    whole(cpart, cpart, osend, csem).wait_send()
    whole(rpart, rpart, osend, rsem).wait_send()
    whole(csum, csum, ssend, ssem).wait_send()
    whole(rsum, rsum, ssend, ssem2).wait_send()


def on_device(points, inv_scale, noise_var, residual, direction):
    vmem = pl.BlockSpec(memory_space=pltpu.VMEM)
    dma = pltpu.SemaphoreType.DMA
    out = jax.ShapeDtypeStruct((R, B), f32)
    return pl.pallas_call(
        kernel,
        out_shape=(out, out),
        in_specs=[pl.BlockSpec(memory_space=pltpu.HBM)] * 5,
        out_specs=(vmem, vmem),
        scratch_shapes=[
            pltpu.VMEM((F, B), f32),
            pltpu.VMEM((1, F), f32),
            pltpu.VMEM((1, B), f32),
            pltpu.VMEM((R, B), f32),
            pltpu.VMEM((R, B), f32),
            pltpu.VMEM((MSG, B), bf16),
            pltpu.VMEM((ROWS - 1, MSG, B), bf16),
            pltpu.VMEM((HALF, MSG, B), bf16),
            pltpu.VMEM((2, DEPTH, WIDTH), bf16),
            pltpu.VMEM((2, R, WIDTH), bf16),
            pltpu.VMEM((2, R, WIDTH), f32),
            pltpu.VMEM((GROUPS, GROUP * B, DEPTH), bf16),
            pltpu.VMEM((GROUPS, R, GROUP * B), bf16),
            pltpu.VMEM((B, DEPTH), bf16),
            pltpu.VMEM((R, B), f32),
            pltpu.VMEM((GROUP * B, WIDTH), bf16),
            pltpu.VMEM((GROUPS, R, GROUP * B), f32),
            pltpu.VMEM((HALF, R, B), f32),
            pltpu.VMEM((ROWS - 1, R, B), f32),
            pltpu.VMEM((1, B), f32),
            pltpu.VMEM((COLS - 1, B), f32),
            pltpu.VMEM((1, B), f32),
            pltpu.VMEM((ROWS - 1, B), f32),
            dma((5,)), dma, dma((ROWS - 1,)), dma((HALF,)), dma, dma, dma, dma, dma, dma,
        ],
        compiler_params=pltpu.CompilerParams(
            collective_id=0, has_side_effects=True, vmem_limit_bytes=60 << 20),
    )(points, inv_scale.reshape(1, F), noise_var.reshape(1, B), residual, direction)


def solution(mesh):
    split_points = P(None, ("row", "col"))
    return jax.shard_map(
        on_device,
        mesh=mesh,
        in_specs=(split_points, P(), P(("row", "col")), split_points, split_points),
        out_specs=(split_points, split_points),
        check_vma=False,
    )
```

time: 61.7 us -> 53.7 us (0.87)
  the two profiles are of different devices: /device:TPU:4 before, /device:TPU:1 now
where the time goes in v3:
time: 53.7 us; the launch traced here: 53.5 us
  Pallas kernels  51 us (95%)
  local copies, waits for them, and re-layouts  1.9 us (4%)
  between operations  0.65 us (1%)
    pallas_call x1, Pallas kernels, on_device(): pl.pallas_call(kernel, out_shape=(out, out), in_specs=[pl.BlockSpec(memor...  51 us
    unnamed x4, local copies, waits for them, and re-layouts  1.9 us

profile of v3, /device:TPU:1, one launch (start us, length us, event | category | flops | bytes accessed | tf_op | source)
XLA Modules:
  0.0 53.5 jit_solution(15060065231875743046)
XLA Ops:
  0.6 51.0 %shard_map.68 = (f32[16,128]{1,0:T(8,128)}, f32[16,128]{1,0:T(8,128)}) custom-call(f32[64,128]{1,0:T(8,128)} %points_hbm.1, f32[1,64]{1,0:T(1,128)} %bitcast.2, f32[1,128]{1,0:T(1,128)} %bitcast.3, f32[16,128]{1,0:T(8,128)} %residual_hbm.1, f32[16,128]{1,0:T(8,128)} %direction_hbm.1), custom_call_target="tpu_custom_call" | custom-call | tf_op jit(solution)/shard_map/pallas_call | solution.py:288
  51.6 0.0 copy-start
  51.6 1.3 %copy.9 = f32[16,128]{1,0:T(8,128)} copy(f32[16,128]{1,0:T(8,128)} %get-tuple-element.4) | data formatting | bytes 16384
  52.9 0.0 copy-done
  52.9 0.6 %copy.10 = f32[16,128]{1,0:T(8,128)} copy(f32[16,128]{1,0:T(8,128)S(1)} %copy-done) | data formatting | bytes 16384
Async XLA Ops:
  51.6 1.3 %copy-start = (f32[16,128]{1,0:T(8,128)S(1)}, f32[16,128]{1,0:T(8,128)}, u32[]{:S(2)}) copy-start(f32[16,128]{1,0:T(8,128)} %get-tuple-element.5) | copy-start | bytes 24580

commit v4 on v3

--- a/solution.py
+++ b/solution.py
@@ -72,7 +72,7 @@
 
 
 def kernel(
-    points_hbm, scale_hbm, noise_hbm, residual_hbm, direction_hbm, res_out, dir_out,
+    points_hbm, scale_hbm, noise_hbm, residual_hbm, direction_hbm, out,
     points, scale, noise, residual, direction, send, jbuf, ibuf, jop, jdir, jacc, iop, idir, oown, own, probs, obuf, cpart, rpart, sums, csum, sums2, rsum,
     in_sem, send_sem, jsem, isem, osend, csem, rsem, ssend, ssem, ssem2,
 ):
@@ -112,23 +112,23 @@
 
     pl.semaphore_wait(barrier, ROWS - 1 + HALF)
 
-    def to_row(d):
-        return pltpu.make_async_remote_copy(
-            src_ref=send, dst_ref=jbuf.at[d - 1], send_sem=send_sem, recv_sem=jsem.at[d - 1],
-            device_id=row_peer(ROWS - d), device_id_type=MESH)
+    def near_first(p):
+        return jnp.where(lax.rem(p, 2) == 1, lax.div(p + 1, 2), lax.rem(ROWS - lax.div(p, 2), ROWS))
+
+    def to_row(p):
+        return pltpu.make_async_remote_copy(
+            src_ref=send, dst_ref=jbuf.at[p], send_sem=send_sem, recv_sem=jsem.at[p],
+            device_id=row_peer(ROWS - near_first(p)), device_id_type=MESH)
 
     def to_col(i):
         return pltpu.make_async_remote_copy(
             src_ref=send, dst_ref=ibuf.at[i - 1], send_sem=send_sem, recv_sem=isem.at[i - 1],
             device_id=col_peer(-shift(i)), device_id_type=MESH)
-
-    def near_first(p):
-        return jnp.where(lax.rem(p, 2) == 1, lax.div(p + 1, 2), lax.rem(ROWS - lax.div(p, 2), ROWS))
 
     def push(k, _):
         @pl.when(k < ROWS)
         def _row():
-            to_row(near_first(k)).start()
+            to_row(k).start()
         to_col(k).start()
         return _
 
@@ -137,25 +137,29 @@
     def slot(n):
         return pl.ds(pl.multiple_of(n * B, B), B)
 
-    def put_j(p, msg):
-        part, place = lax.div(p, ROWS // 2), slot(lax.rem(p, ROWS // 2))
-        jop[part, :, place] = j_operand(decode(msg[:F], factor))
-        jdir[part, :, place] = msg[F:]
-
-    def take_j(p, _):
-        d = near_first(p)
-        to_row(d).wait_recv()
-        put_j(p, jbuf[d - 1])
-        return _
-
-    def take_i(n, g):
-        i = g * GROUP + n
-        to_col(i + 1).wait_recv()
-        msg = ibuf[i]
-        weight = jnp.where(i == HALF - 1, 0.5, 1.0)
-        iop[g, slot(n), :] = i_operand(decode(msg[:F], factor))
-        idir[g, :, slot(n)] = (msg[F:].astype(f32) * weight).astype(bf16)
-        return g
+    def side_by_side(blocks):
+        return jnp.concatenate(blocks, axis=1)
+
+    def take_j(q, _):
+        for n in range(GROUP):
+            @pl.when(q * GROUP + n > 0)
+            def _arrived():
+                to_row(q * GROUP + n).wait_recv()
+        part = lax.div(q, 2)
+        place = pl.ds(pl.multiple_of(lax.rem(q, 2) * GROUP * B, GROUP * B), GROUP * B)
+        blocks = [jbuf[q * GROUP + n] for n in range(GROUP)]
+        jop[part, :, place] = j_operand(decode(side_by_side([m[:F] for m in blocks]), factor))
+        jdir[part, :, place] = side_by_side([m[F:] for m in blocks])
+        return _
+
+    def take_i(g):
+        for n in range(GROUP):
+            to_col(g * GROUP + n + 1).wait_recv()
+        weight = jnp.where(g == GROUPS - 1, 0.5, 1.0)
+        blocks = [ibuf[g * GROUP + n] for n in range(GROUP)]
+        iop[g] = i_operand(decode(side_by_side([m[:F] for m in blocks]), factor))
+        last = (blocks[-1][F:].astype(f32) * weight).astype(bf16)
+        idir[g] = side_by_side([m[F:] for m in blocks[:-1]] + [last])
 
     def tile(left, dirs_i, h, probs):
         for n in range(WIDTH // CHUNK):
@@ -185,7 +189,7 @@
         to_row_owner(p).start()
         return _
 
-    put_j(0, send[...])
+    jbuf[0] = send[...]
     oown[...] = i_operand(decode(send[:F], factor))
     jacc[...] = jnp.zeros(jacc.shape, f32)
     obuf[...] = jnp.zeros(obuf.shape, f32)
@@ -198,12 +202,12 @@
 
         @pl.when(early & (lax.rem(t, 2) == 0))
         def _half():
-            lax.fori_loop(jnp.maximum(h * (ROWS // 2), 1), (h + 1) * (ROWS // 2), take_j, 0)
+            lax.fori_loop(2 * h, 2 * h + 2, take_j, 0)
             own[...] += 0.5 * tile(oown[...], send[F:] * bf16(0.5), h, probs.at[:B])
 
         @pl.when(h == 0)
         def _group():
-            lax.fori_loop(0, GROUP, take_i, g)
+            take_i(g)
 
         obuf[g] += tile(iop[g], idir[g], h, probs)
 
@@ -269,11 +273,11 @@
     rr, rq, dq, qq = (jnp.sum(jnp.where(ahead == n * R, tot, 0.0), axis=1, keepdims=True) for n in range(4))
     step = rr / dq
     nxt = rr - 2.0 * step * rq + step * (step * qq)
-    res_next = res - step * image
-    res_out[...] = res_next
-    dir_out[...] = res_next + (nxt / rr) * dirs
-
-    whole(jbuf, jbuf, send_sem, jsem.at[0]).wait_send()
+    out[:R, :] = image
+    out[R:2 * R, :] = jnp.broadcast_to(step, (R, B))
+    out[2 * R:, :] = jnp.broadcast_to(nxt / rr, (R, B))
+
+    whole(jbuf.at[pl.ds(1, ROWS - 1)], jbuf.at[pl.ds(1, ROWS - 1)], send_sem, jsem.at[0]).wait_send()
     whole(ibuf, ibuf, send_sem, jsem.at[0]).wait_send()
     whole(cpart, cpart, osend, csem).wait_send()
     whole(rpart, rpart, osend, rsem).wait_send()
@@ -284,12 +288,11 @@
 def on_device(points, inv_scale, noise_var, residual, direction):
     vmem = pl.BlockSpec(memory_space=pltpu.VMEM)
     dma = pltpu.SemaphoreType.DMA
-    out = jax.ShapeDtypeStruct((R, B), f32)
-    return pl.pallas_call(
+    found = pl.pallas_call(
         kernel,
-        out_shape=(out, out),
+        out_shape=jax.ShapeDtypeStruct((3 * R, B), f32),
         in_specs=[pl.BlockSpec(memory_space=pltpu.HBM)] * 5,
-        out_specs=(vmem, vmem),
+        out_specs=vmem,
         scratch_shapes=[
             pltpu.VMEM((F, B), f32),
             pltpu.VMEM((1, F), f32),
@@ -297,7 +300,7 @@
             pltpu.VMEM((R, B), f32),
             pltpu.VMEM((R, B), f32),
             pltpu.VMEM((MSG, B), bf16),
-            pltpu.VMEM((ROWS - 1, MSG, B), bf16),
+            pltpu.VMEM((ROWS, MSG, B), bf16),
             pltpu.VMEM((HALF, MSG, B), bf16),
             pltpu.VMEM((2, DEPTH, WIDTH), bf16),
             pltpu.VMEM((2, R, WIDTH), bf16),
@@ -314,11 +317,14 @@
             pltpu.VMEM((COLS - 1, B), f32),
             pltpu.VMEM((1, B), f32),
             pltpu.VMEM((ROWS - 1, B), f32),
-            dma((5,)), dma, dma((ROWS - 1,)), dma((HALF,)), dma, dma, dma, dma, dma, dma,
+            dma((5,)), dma, dma((ROWS,)), dma((HALF,)), dma, dma, dma, dma, dma, dma,
         ],
         compiler_params=pltpu.CompilerParams(
             collective_id=0, has_side_effects=True, vmem_limit_bytes=60 << 20),
     )(points, inv_scale.reshape(1, F), noise_var.reshape(1, B), residual, direction)
+    image, step, ratio = found[:R], found[R:2 * R], found[2 * R:]
+    residual_next = residual - step * image
+    return residual_next, residual_next + ratio * direction
 
 
 def solution(mesh):

time: 53.7 us -> 52.2 us (0.972)
  local copies, waits for them, and re-layouts: 1.9 us -> 0.01 us
  other arithmetic: 0 us -> 1.34 us
  Pallas kernels: 51 us -> 49.9 us
    unnamed x4, local copies, waits for them, and re-layouts: 1.9 us -> 0.01 us
    add x0 -> x1, other arithmetic: none -> 1.34 us  [on_device(): return (residual_next, residual_next + ratio * direction)]
    pallas_call x1, Pallas kernels: 51 us -> 49.9 us  [on_device(): pl.pallas_call(kernel, out_shape=jax.ShapeDtypeStruct((3 * R, B), f32), i...]
where the time goes in v4:
time: 52.2 us; the launch traced here: 51.9 us
  Pallas kernels  49.9 us (96%)
  other arithmetic  1.34 us (3%)
  between operations  0.67 us (1%)
    pallas_call x1, Pallas kernels, on_device(): pl.pallas_call(kernel, out_shape=jax.ShapeDtypeStruct((3 * R, B), f32), i...  49.9 us
    add x1, other arithmetic, on_device(): return (residual_next, residual_next + ratio * direction)  1.34 us

profile of v4, /device:TPU:1, one launch (start us, length us, event | category | flops | bytes accessed | tf_op | source)
XLA Modules:
  0.0 51.9 jit_solution(6978655548760067602)
XLA Ops:
  0.6 0.0 copy-start
  0.6 0.0 copy-start.1
  0.7 49.9 %shard_map.68 = f32[48,128]{1,0:T(8,128)} custom-call(f32[64,128]{1,0:T(8,128)} %points_hbm.1, f32[1,64]{1,0:T(1,128)} %bitcast.2, f32[1,128]{1,0:T(1,128)} %bitcast.3, f32[16,128]{1,0:T(8,128)} %residual_hbm.1, f32[16,128]{1,0:T(8,128)} %direction_hbm.1), custom_call_target="tpu_custom_call" | custom-call | tf_op jit(solution)/shard_map/pallas_call | solution.py:291
  50.6 0.0 copy-done
  50.6 0.0 copy-done.1
  50.6 1.3 %multiply_add_fusion = (f32[16,128]{1,0:T(8,128)}, f32[16,128]{1,0:T(8,128)}) fusion(f32[16,128]{1,0:T(8,128)S(1)} %copy-done, f32[48,128]{1,0:T(8,128)} %shard_map.68, f32[16,128]{1,0:T(8,128)S(1)} %copy-done.1), kind=kLoop, calls=%fused_computation | loop fusion | flops 8192 | bytes 57344 | tf_op jit(solution)/shard_map/add | solution.py:327
Async XLA Ops:
  0.6 49.9 %copy-start = (f32[16,128]{1,0:T(8,128)S(1)}, f32[16,128]{1,0:T(8,128)}, u32[]{:S(2)}) copy-start(f32[16,128]{1,0:T(8,128)} %direction_hbm.1) | copy-start | bytes 24580
  0.6 49.9 %copy-start.1 = (f32[16,128]{1,0:T(8,128)S(1)}, f32[16,128]{1,0:T(8,128)}, u32[]{:S(2)}) copy-start(f32[16,128]{1,0:T(8,128)} %residual_hbm.1) | copy-start | bytes 24580

commit v5 on v4

--- a/solution.py
+++ b/solution.py
@@ -85,7 +85,8 @@
         return (r, lax.rem(c + d + COLS, COLS))
 
     def shift(i):
-        return jnp.where(lax.rem(i, 2) == 1, i, -i)
+        d = HALF + 1 - i
+        return jnp.where(lax.rem(d, 2) == 1, d, -d)
 
     staged = ((points_hbm, points), (scale_hbm, scale), (noise_hbm, noise), (residual_hbm, residual), (direction_hbm, direction))
     for n, (src, dst) in enumerate(staged):
@@ -97,11 +98,10 @@
         @pl.when(k < ROWS)
         def _row():
             pl.semaphore_signal(barrier, inc=1, device_id=row_peer(far_first(k, ROWS)), device_id_type=MESH)
-        i = HALF + 1 - k
-        pl.semaphore_signal(barrier, inc=1, device_id=col_peer(shift(i)), device_id_type=MESH)
-        return _
-
-    lax.fori_loop(1, HALF + 1, greet, 0)
+        pl.semaphore_signal(barrier, inc=1, device_id=col_peer(shift(k)), device_id_type=MESH)
+        return _
+
+    lax.fori_loop(1, HALF + 1, greet, 0, unroll=True)
 
     for n, (src, dst) in enumerate(staged):
         pltpu.make_async_copy(src, dst, in_sem.at[n]).wait()
@@ -112,13 +112,10 @@
 
     pl.semaphore_wait(barrier, ROWS - 1 + HALF)
 
-    def near_first(p):
-        return jnp.where(lax.rem(p, 2) == 1, lax.div(p + 1, 2), lax.rem(ROWS - lax.div(p, 2), ROWS))
-
     def to_row(p):
         return pltpu.make_async_remote_copy(
             src_ref=send, dst_ref=jbuf.at[p], send_sem=send_sem, recv_sem=jsem.at[p],
-            device_id=row_peer(ROWS - near_first(p)), device_id_type=MESH)
+            device_id=row_peer(ROWS - far_first(p, ROWS)), device_id_type=MESH)
 
     def to_col(i):
         return pltpu.make_async_remote_copy(
@@ -132,7 +129,7 @@
         to_col(k).start()
         return _
 
-    lax.fori_loop(1, HALF + 1, push, 0)
+    lax.fori_loop(1, HALF + 1, push, 0, unroll=True)
 
     def slot(n):
         return pl.ds(pl.multiple_of(n * B, B), B)
@@ -155,11 +152,11 @@
     def take_i(g):
         for n in range(GROUP):
             to_col(g * GROUP + n + 1).wait_recv()
-        weight = jnp.where(g == GROUPS - 1, 0.5, 1.0)
+        weight = jnp.where(g == 0, 0.5, 1.0)
         blocks = [ibuf[g * GROUP + n] for n in range(GROUP)]
         iop[g] = i_operand(decode(side_by_side([m[:F] for m in blocks]), factor))
-        last = (blocks[-1][F:].astype(f32) * weight).astype(bf16)
-        idir[g] = side_by_side([m[F:] for m in blocks[:-1]] + [last])
+        first = (blocks[0][F:].astype(f32) * weight).astype(bf16)
+        idir[g] = side_by_side([first] + [m[F:] for m in blocks[1:]])
 
     def tile(left, dirs_i, h, probs):
         for n in range(WIDTH // CHUNK):
@@ -180,7 +177,7 @@
         return g
 
     def to_row_owner(p):
-        d = near_first(p)
+        d = far_first(p, ROWS)
         return pltpu.make_async_remote_copy(
             src_ref=jacc.at[lax.div(p, ROWS // 2), :, slot(lax.rem(p, ROWS // 2))], dst_ref=rpart.at[d - 1],
             send_sem=osend, recv_sem=rsem, device_id=row_peer(d), device_id_type=MESH)
@@ -196,11 +193,9 @@
     own[...] = jnp.zeros(own.shape, f32)
 
     def step_of(t, _):
-        early = t < GROUPS
-        g = jnp.where(early, lax.rem(t, 2), lax.div(t, 2))
-        h = jnp.where(early, lax.div(t, 2), lax.rem(t, 2))
-
-        @pl.when(early & (lax.rem(t, 2) == 0))
+        g, h = lax.rem(t, GROUPS), lax.div(t, GROUPS)
+
+        @pl.when(g == 0)
         def _half():
             lax.fori_loop(2 * h, 2 * h + 2, take_j, 0)
             own[...] += 0.5 * tile(oown[...], send[F:] * bf16(0.5), h, probs.at[:B])
@@ -211,15 +206,15 @@
 
         obuf[g] += tile(iop[g], idir[g], h, probs)
 
-        @pl.when(t == 2 * GROUPS - 1)
-        def _last():
-            obuf[g, :, slot(GROUP - 1)] = 0.5 * obuf[g, :, slot(GROUP - 1)]
+        @pl.when(t == GROUPS)
+        def _half_weight():
+            obuf[0, :, :B] = 0.5 * obuf[0, :, :B]
 
         @pl.when(h == 1)
         def _rows_done():
             lax.fori_loop(0, GROUP, push_o, g)
 
-        @pl.when(t >= 2 * GROUPS - 2)
+        @pl.when(g == GROUPS - 1)
         def _columns_done():
             lax.fori_loop(jnp.maximum(h * (ROWS // 2), 1), (h + 1) * (ROWS // 2), push_j, 0)
         return _
@@ -254,7 +249,7 @@
         sum_to_col(far_first(k, COLS)).start()
         return _
 
-    lax.fori_loop(1, COLS, push_c, 0)
+    lax.fori_loop(1, COLS, push_c, 0, unroll=True)
     whole(csum, csum, ssend, ssem).wait_recv()
     sums2[...] = sums[...] + jnp.sum(csum[...], axis=0, keepdims=True)
 
@@ -267,7 +262,7 @@
         sum_to_row(far_first(k, ROWS)).start()
         return _
 
-    lax.fori_loop(1, ROWS, push_r, 0)
+    lax.fori_loop(1, ROWS, push_r, 0, unroll=True)
     whole(rsum, rsum, ssend, ssem2).wait_recv()
     tot = sums2[...] + jnp.sum(rsum[...], axis=0, keepdims=True)
     rr, rq, dq, qq = (jnp.sum(jnp.where(ahead == n * R, tot, 0.0), axis=1, keepdims=True) for n in range(4))

time: 52.2 us -> 50.9 us (0.975)
  Pallas kernels: 49.9 us -> 48.6 us
    pallas_call x1, Pallas kernels: 49.9 us -> 48.6 us  [on_device(): pl.pallas_call(kernel, out_shape=jax.ShapeDtypeStruct((3 * R, B), f32), i...]
where the time goes in v5:
time: 50.9 us; the launch traced here: 50.6 us
  Pallas kernels  48.6 us (95%)
  other arithmetic  1.34 us (3%)
  between operations  0.67 us (1%)
    pallas_call x1, Pallas kernels, on_device(): pl.pallas_call(kernel, out_shape=jax.ShapeDtypeStruct((3 * R, B), f32), i...  48.6 us
    add x1, other arithmetic, on_device(): return (residual_next, residual_next + ratio * direction)  1.34 us

profile of v5, /device:TPU:1, one launch (start us, length us, event | category | flops | bytes accessed | tf_op | source)
XLA Modules:
  0.0 50.6 jit_solution(9130761414136349671)
XLA Ops:
  0.6 0.0 copy-start
  0.6 0.0 copy-start.1
  0.7 48.6 %shard_map.68 = f32[48,128]{1,0:T(8,128)} custom-call(f32[64,128]{1,0:T(8,128)} %points_hbm.1, f32[1,64]{1,0:T(1,128)} %bitcast.2, f32[1,128]{1,0:T(1,128)} %bitcast.3, f32[16,128]{1,0:T(8,128)} %residual_hbm.1, f32[16,128]{1,0:T(8,128)} %direction_hbm.1), custom_call_target="tpu_custom_call" | custom-call | tf_op jit(solution)/shard_map/pallas_call | solution.py:286
  49.3 0.0 copy-done
  49.3 0.0 copy-done.1
  49.3 1.3 %multiply_add_fusion = (f32[16,128]{1,0:T(8,128)}, f32[16,128]{1,0:T(8,128)}) fusion(f32[16,128]{1,0:T(8,128)S(1)} %copy-done, f32[48,128]{1,0:T(8,128)} %shard_map.68, f32[16,128]{1,0:T(8,128)S(1)} %copy-done.1), kind=kLoop, calls=%fused_computation | loop fusion | flops 8192 | bytes 57344 | tf_op jit(solution)/shard_map/add | solution.py:322
Async XLA Ops:
  0.6 48.7 %copy-start = (f32[16,128]{1,0:T(8,128)S(1)}, f32[16,128]{1,0:T(8,128)}, u32[]{:S(2)}) copy-start(f32[16,128]{1,0:T(8,128)} %direction_hbm.1) | copy-start | bytes 24580
  0.6 48.7 %copy-start.1 = (f32[16,128]{1,0:T(8,128)S(1)}, f32[16,128]{1,0:T(8,128)}, u32[]{:S(2)}) copy-start(f32[16,128]{1,0:T(8,128)} %residual_hbm.1) | copy-start | bytes 24580

commit v6 on v5

--- a/solution.py
+++ b/solution.py
@@ -285,7 +285,7 @@
     dma = pltpu.SemaphoreType.DMA
     found = pl.pallas_call(
         kernel,
-        out_shape=jax.ShapeDtypeStruct((3 * R, B), f32),
+        out_shape=pltpu.VMEM((3 * R, B), f32),
         in_specs=[pl.BlockSpec(memory_space=pltpu.HBM)] * 5,
         out_specs=vmem,
         scratch_shapes=[

time: 50.9 us -> 49.5 us (0.972)
  other arithmetic: 1.34 us -> 0.61 us
  Pallas kernels: 48.6 us -> 48 us
    add x1, other arithmetic: 1.34 us -> 0.61 us  [on_device(): return (residual_next, residual_next + ratio * direction)]
    pallas_call x1, Pallas kernels: 48.6 us -> 48 us  [on_device(): pl.pallas_call(kernel, out_shape=pltpu.VMEM((3 * R, B), f32), in_specs=[p...]
where the time goes in v6:
time: 49.5 us; the launch traced here: 49.3 us
  Pallas kernels  48 us (97%)
  between operations  0.67 us (1%)
  other arithmetic  0.61 us (1%)
    pallas_call x1, Pallas kernels, on_device(): pl.pallas_call(kernel, out_shape=pltpu.VMEM((3 * R, B), f32), in_specs=[p...  48 us

profile of v6, /device:TPU:1, one launch (start us, length us, event | category | flops | bytes accessed | tf_op | source)
XLA Modules:
  0.0 49.3 jit_solution(6920054849316649673)
XLA Ops:
  0.6 0.0 copy-start
  0.6 0.0 copy-start.1
  0.7 48.0 %shard_map.68 = f32[48,128]{1,0:T(8,128)S(1)} custom-call(f32[64,128]{1,0:T(8,128)} %points_hbm.1, f32[1,64]{1,0:T(1,128)} %bitcast.2, f32[1,128]{1,0:T(1,128)} %bitcast.3, f32[16,128]{1,0:T(8,128)} %residual_hbm.1, f32[16,128]{1,0:T(8,128)} %direction_hbm.1), custom_call_target="tpu_custom_call" | custom-call | tf_op jit(solution)/shard_map/pallas_call | solution.py:286
  48.7 0.0 copy-done
  48.7 0.0 copy-done.1
  48.7 0.6 %multiply_add_fusion = (f32[16,128]{1,0:T(8,128)}, f32[16,128]{1,0:T(8,128)}) fusion(f32[16,128]{1,0:T(8,128)S(1)} %copy-done, f32[48,128]{1,0:T(8,128)S(1)} %shard_map.68, f32[16,128]{1,0:T(8,128)S(1)} %copy-done.1), kind=kLoop, calls=%fused_computation | loop fusion | flops 8192 | bytes 57344 | tf_op jit(solution)/shard_map/add | solution.py:322
Async XLA Ops:
  0.6 48.0 %copy-start = (f32[16,128]{1,0:T(8,128)S(1)}, f32[16,128]{1,0:T(8,128)}, u32[]{:S(2)}) copy-start(f32[16,128]{1,0:T(8,128)} %direction_hbm.1) | copy-start | bytes 24580
  0.6 48.0 %copy-start.1 = (f32[16,128]{1,0:T(8,128)S(1)}, f32[16,128]{1,0:T(8,128)}, u32[]{:S(2)}) copy-start(f32[16,128]{1,0:T(8,128)} %residual_hbm.1) | copy-start | bytes 24580

commit v7 on v6

--- a/solution.py
+++ b/solution.py
@@ -19,7 +19,7 @@
 KEEP = 48
 GROUP, GROUPS = 4, 4
 WIDTH = ROWS * B // 2
-CHUNK = 512
+CHUNK = 256
 CODE = 250.0 / 6.0
 BIAS = 125.0
 SQRT_LOG2E = math.sqrt(math.log2(math.e))
@@ -222,6 +222,8 @@
     lax.fori_loop(0, 2 * GROUPS, step_of, 0)
 
     res = residual[...]
+    ahead = lax.broadcasted_iota(jnp.int32, (R, B), 1) - lax.broadcasted_iota(jnp.int32, (R, B), 0)
+    local = jnp.where(ahead == 0, jnp.sum(res * res, axis=1, keepdims=True), 0.0)
     total = own[...] + jacc[0, :, :B] + noise[...] * dirs
 
     def whole(src, dst, s_sem, r_sem):
@@ -234,9 +236,7 @@
     whole(rpart, rpart, osend, rsem).wait_recv()
     image = total + jnp.sum(rpart[...], axis=0)
 
-    ahead = lax.broadcasted_iota(jnp.int32, (R, B), 1) - lax.broadcasted_iota(jnp.int32, (R, B), 0)
-    local = jnp.zeros((R, B), f32)
-    for n, prod in enumerate((res * res, res * image, dirs * image, image * image)):
+    for n, prod in enumerate((res * image, dirs * image, image * image), 1):
         local = jnp.where(ahead == n * R, jnp.sum(prod, axis=1, keepdims=True), local)
     sums[...] = jnp.sum(local, axis=0, keepdims=True)
 

time: 49.5 us -> 49.5 us (level)
  no operation moved by 1% of the time
where the time goes in v7:
time: 49.5 us; the launch traced here: 49.3 us
  Pallas kernels  48 us (97%)
  between operations  0.67 us (1%)
  other arithmetic  0.61 us (1%)
    pallas_call x1, Pallas kernels, on_device(): pl.pallas_call(kernel, out_shape=pltpu.VMEM((3 * R, B), f32), in_specs=[p...  48 us

profile of v7, /device:TPU:1, one launch (start us, length us, event | category | flops | bytes accessed | tf_op | source)
XLA Modules:
  0.0 49.3 jit_solution(16762805877382725718)
XLA Ops:
  0.6 0.0 copy-start
  0.6 0.0 copy-start.1
  0.7 48.0 %shard_map.68 = f32[48,128]{1,0:T(8,128)S(1)} custom-call(f32[64,128]{1,0:T(8,128)} %points_hbm.1, f32[1,64]{1,0:T(1,128)} %bitcast.2, f32[1,128]{1,0:T(1,128)} %bitcast.3, f32[16,128]{1,0:T(8,128)} %residual_hbm.1, f32[16,128]{1,0:T(8,128)} %direction_hbm.1), custom_call_target="tpu_custom_call" | custom-call | tf_op jit(solution)/shard_map/pallas_call | solution.py:286
  48.7 0.0 copy-done
  48.7 0.0 copy-done.1
  48.7 0.6 %multiply_add_fusion = (f32[16,128]{1,0:T(8,128)}, f32[16,128]{1,0:T(8,128)}) fusion(f32[16,128]{1,0:T(8,128)S(1)} %copy-done, f32[48,128]{1,0:T(8,128)S(1)} %shard_map.68, f32[16,128]{1,0:T(8,128)S(1)} %copy-done.1), kind=kLoop, calls=%fused_computation | loop fusion | flops 8192 | bytes 57344 | tf_op jit(solution)/shard_map/add | solution.py:322
Async XLA Ops:
  0.6 48.0 %copy-start = (f32[16,128]{1,0:T(8,128)S(1)}, f32[16,128]{1,0:T(8,128)}, u32[]{:S(2)}) copy-start(f32[16,128]{1,0:T(8,128)} %direction_hbm.1) | copy-start | bytes 24580
  0.6 48.0 %copy-start.1 = (f32[16,128]{1,0:T(8,128)S(1)}, f32[16,128]{1,0:T(8,128)}, u32[]{:S(2)}) copy-start(f32[16,128]{1,0:T(8,128)} %residual_hbm.1) | copy-start | bytes 24580

commit v8 on v6

--- a/solution.py
+++ b/solution.py
@@ -88,10 +88,6 @@
         d = HALF + 1 - i
         return jnp.where(lax.rem(d, 2) == 1, d, -d)
 
-    staged = ((points_hbm, points), (scale_hbm, scale), (noise_hbm, noise), (residual_hbm, residual), (direction_hbm, direction))
-    for n, (src, dst) in enumerate(staged):
-        pltpu.make_async_copy(src, dst, in_sem.at[n]).start()
-
     barrier = pltpu.get_barrier_semaphore()
 
     def greet(k, _):
@@ -102,6 +98,10 @@
         return _
 
     lax.fori_loop(1, HALF + 1, greet, 0, unroll=True)
+
+    staged = ((points_hbm, points), (scale_hbm, scale), (noise_hbm, noise), (residual_hbm, residual), (direction_hbm, direction))
+    for n, (src, dst) in enumerate(staged):
+        pltpu.make_async_copy(src, dst, in_sem.at[n]).start()
 
     for n, (src, dst) in enumerate(staged):
         pltpu.make_async_copy(src, dst, in_sem.at[n]).wait()
@@ -189,37 +189,44 @@
     jbuf[0] = send[...]
     oown[...] = i_operand(decode(send[:F], factor))
     jacc[...] = jnp.zeros(jacc.shape, f32)
-    obuf[...] = jnp.zeros(obuf.shape, f32)
     own[...] = jnp.zeros(own.shape, f32)
 
-    def step_of(t, _):
-        g, h = lax.rem(t, GROUPS), lax.div(t, GROUPS)
-
-        @pl.when(g == 0)
-        def _half():
-            lax.fori_loop(2 * h, 2 * h + 2, take_j, 0)
-            own[...] += 0.5 * tile(oown[...], send[F:] * bf16(0.5), h, probs.at[:B])
-
-        @pl.when(h == 0)
-        def _group():
-            take_i(g)
-
-        obuf[g] += tile(iop[g], idir[g], h, probs)
-
-        @pl.when(t == GROUPS)
+    def half_of_j(h):
+        lax.fori_loop(2 * h, 2 * h + 2, take_j, 0)
+        own[...] += 0.5 * tile(oown[...], send[F:] * bf16(0.5), h, probs.at[:B])
+
+    def push_half(h):
+        for p in range(max(h * (ROWS // 2), 1), (h + 1) * (ROWS // 2)):
+            push_j(p, 0)
+
+    def one_group(g, _):
+        take_i(g)
+        obuf[g] = tile(iop[g], idir[g], 0, probs.at[:GROUP * B])
+        return _
+
+    def two_groups(u, _):
+        g = 2 * u
+        left = jnp.concatenate([iop[g], iop[g + 1]], axis=0)
+        out = tile(left, side_by_side([idir[g], idir[g + 1]]), 1, probs)
+        obuf[g] += out[:, :GROUP * B]
+        obuf[g + 1] += out[:, GROUP * B:]
+
+        @pl.when(u == 0)
         def _half_weight():
             obuf[0, :, :B] = 0.5 * obuf[0, :, :B]
 
-        @pl.when(h == 1)
-        def _rows_done():
-            lax.fori_loop(0, GROUP, push_o, g)
-
-        @pl.when(g == GROUPS - 1)
-        def _columns_done():
-            lax.fori_loop(jnp.maximum(h * (ROWS // 2), 1), (h + 1) * (ROWS // 2), push_j, 0)
-        return _
-
-    lax.fori_loop(0, 2 * GROUPS, step_of, 0)
+        for n in range(GROUP):
+            push_o(n, g)
+        for n in range(GROUP):
+            push_o(n, g + 1)
+        return _
+
+    half_of_j(0)
+    lax.fori_loop(0, GROUPS, one_group, 0)
+    push_half(0)
+    half_of_j(1)
+    lax.fori_loop(0, GROUPS // 2, two_groups, 0)
+    push_half(1)
 
     res = residual[...]
     total = own[...] + jacc[0, :, :B] + noise[...] * dirs
@@ -304,7 +311,7 @@
             pltpu.VMEM((GROUPS, R, GROUP * B), bf16),
             pltpu.VMEM((B, DEPTH), bf16),
             pltpu.VMEM((R, B), f32),
-            pltpu.VMEM((GROUP * B, WIDTH), bf16),
+            pltpu.VMEM((2 * GROUP * B, WIDTH), bf16),
             pltpu.VMEM((GROUPS, R, GROUP * B), f32),
             pltpu.VMEM((HALF, R, B), f32),
             pltpu.VMEM((ROWS - 1, R, B), f32),

time: 49.5 us -> 50 us (1.010)
  Pallas kernels: 48 us -> 48.5 us
    pallas_call x1, Pallas kernels: 48 us -> 48.5 us  [on_device(): pl.pallas_call(kernel, out_shape=pltpu.VMEM((3 * R, B), f32), in_specs=[p...]
where the time goes in v8:
time: 50 us; the launch traced here: 49.8 us
  Pallas kernels  48.5 us (97%)
  between operations  0.67 us (1%)
  other arithmetic  0.61 us (1%)
    pallas_call x1, Pallas kernels, on_device(): pl.pallas_call(kernel, out_shape=pltpu.VMEM((3 * R, B), f32), in_specs=[p...  48.5 us

profile of v8, /device:TPU:1, one launch (start us, length us, event | category | flops | bytes accessed | tf_op | source)
XLA Modules:
  0.0 49.8 jit_solution(7009564677003930594)
XLA Ops:
  0.6 0.0 copy-start
  0.6 0.0 copy-start.1
  0.7 48.5 %shard_map.68 = f32[48,128]{1,0:T(8,128)S(1)} custom-call(f32[64,128]{1,0:T(8,128)} %points_hbm.1, f32[1,64]{1,0:T(1,128)} %bitcast.2, f32[1,128]{1,0:T(1,128)} %bitcast.3, f32[16,128]{1,0:T(8,128)} %residual_hbm.1, f32[16,128]{1,0:T(8,128)} %direction_hbm.1), custom_call_target="tpu_custom_call" | custom-call | tf_op jit(solution)/shard_map/pallas_call | solution.py:293
  49.2 0.0 copy-done
  49.2 0.0 copy-done.1
  49.2 0.6 %multiply_add_fusion = (f32[16,128]{1,0:T(8,128)}, f32[16,128]{1,0:T(8,128)}) fusion(f32[16,128]{1,0:T(8,128)S(1)} %copy-done, f32[48,128]{1,0:T(8,128)S(1)} %shard_map.68, f32[16,128]{1,0:T(8,128)S(1)} %copy-done.1), kind=kLoop, calls=%fused_computation | loop fusion | flops 8192 | bytes 57344 | tf_op jit(solution)/shard_map/add | solution.py:329
Async XLA Ops:
  0.6 48.6 %copy-start = (f32[16,128]{1,0:T(8,128)S(1)}, f32[16,128]{1,0:T(8,128)}, u32[]{:S(2)}) copy-start(f32[16,128]{1,0:T(8,128)} %direction_hbm.1) | copy-start | bytes 24580
  0.6 48.6 %copy-start.1 = (f32[16,128]{1,0:T(8,128)S(1)}, f32[16,128]{1,0:T(8,128)}, u32[]{:S(2)}) copy-start(f32[16,128]{1,0:T(8,128)} %residual_hbm.1) | copy-start | bytes 24580
